TPU v7x, 128 devices: a whole 4x4x4 slice. The times are simulated.
128 devices in a mesh: vocab: 32 (over z, y, core), batch: 4 (over x).
Axes of the slice: x: 4, y: 4, z: 4, core: 2. Of those that a mesh axis runs over, the one named last changes fastest.
Arguments:
- hidden: bfloat16 [6144, 7168], P(('batch', 'vocab')), parts along dimension 0
- head_codes: bfloat16 [131072, 7168], P(('batch', 'vocab')), parts along dimension 0, may hold values from -4 to 4
- head_scales: float32 [1024, 56], P(('batch', 'vocab')), parts along dimension 0, may hold values from 0.01 to 0.1
Outputs:
- probabilities: bfloat16 [6144, 32768], P(('batch', 'vocab')), parts along dimension 0
- entropy: float32 [6144], P(('batch', 'vocab')), parts along dimension 0
There are 4 independent parts, one for each index of `batch`. A program takes and returns all parts, laid end to end along the dimension named above; each array names one. Nothing has to cross between parts.
All inputs are finite; a program needn't handle non-finite values.
Results may differ from a plain program's by a relative error of at most 0.0098.
Values may be sent and summed in bfloat16 or wider, within the bound.
A program may use at most 192 MiB of HBM per device.

v0:
```python
import jax
import jax.numpy as jnp
from jax import lax
from jax.sharding import PartitionSpec as P


def shards(hidden, head_codes, head_scales):
    vocab_rows, model_width = head_codes.shape
    owned_rows = hidden.shape[0]
    grouped = head_codes.reshape(vocab_rows // 128, 128, model_width // 128, 128).astype(
        jnp.float32
    )
    weight = (
        (grouped * head_scales[:, None, :, None])
        .reshape(vocab_rows, model_width)
        .astype(jnp.bfloat16)
    )
    logits = lax.dot_general(
        lax.all_gather(hidden, "vocab", axis=0, tiled=True),
        weight,
        (((1,), (1,)), ((), ())),
        preferred_element_type=jnp.float32,
    )
    local_top = jnp.max(logits, axis=1)
    local_shift = logits - local_top[:, None]
    local_expf = jnp.exp(local_shift)
    local_sum = jnp.sum(local_expf, axis=1)
    local_tilt = jnp.sum(local_expf * local_shift, axis=1)
    local_exp = lax.optimization_barrier(local_expf.astype(jnp.bfloat16))
    top_value = lax.pmax(local_top, "vocab")
    factor = jnp.exp(local_top - top_value)
    exp_sum, tilt_sum = lax.psum(
        (local_sum * factor, factor * (local_tilt + local_sum * (local_top - top_value))), "vocab"
    )
    spread = (local_exp.astype(jnp.float32) * (factor / exp_sum)[:, None]).astype(jnp.bfloat16)
    probabilities = lax.all_to_all(spread, "vocab", split_axis=0, concat_axis=1, tiled=True)
    offset = lax.axis_index("vocab") * owned_rows
    owned_sum = lax.dynamic_slice_in_dim(exp_sum, offset, owned_rows, 0)
    owned_tilt = lax.dynamic_slice_in_dim(tilt_sum, offset, owned_rows, 0)
    entropy = jnp.log(owned_sum) - owned_tilt / owned_sum
    return (probabilities, entropy)


def solution(mesh):
    placed = (P(("batch", "vocab"), None), P(("batch", "vocab"), None), P(("batch", "vocab"), None))
    return jax.shard_map(
        shards,
        mesh=mesh,
        in_specs=placed,
        out_specs=(P(("batch", "vocab"), None), P(("batch", "vocab"))),
        check_vma=False,
    )
```

profile of v0, /device:TPU:1, one launch (start us, length us, event | category | flops | bytes accessed | tf_op | source)
XLA Modules:
  0.0 400.0 jit_solution(17090052432900826863)
XLA Ops:
  7.2 0.0 all-gather.2.cloned.1.call-start
  7.2 0.7 all-gather.2.cloned.1.call-update
  7.9 90.9 %all-gather.2.cloned.1.call-done = bf16[1536,7168]{1,0:T(8,128)(2,1)} async-done(((bf16[48,7168]{1,0:T(8,128)(2,1)}), bf16[1536,7168]{1,0:T(8,128)(2,1)}) %all-gather.2.cloned.1.call-update) | async-done | bytes 22020112 | tf_op jit(solution)/shard_map/all_gather | solution.py:19
  98.8 12.3 %mul.34 = f32[8,128,56,128]{3,2,1,0:T(8,128)} broadcast(f32[8,56]{1,0:T(8,128)} %param.5), dimensions={0,2} | broadcast | bytes 29361920 | tf_op jit(solution)/shard_map/mul | solution.py:14
  111.1 35.2 %fusion.4 = (f32[1536]{0:T(1024)S(1)}, f32[1024,1536]{1,0:T(8,128)}) fusion(bf16[1536,7168]{1,0:T(8,128)(2,1)} %all-gather.2.cloned.1.call-done, f32[128,8,56,128]{3,2,1,0:T(8,128)} %bitcast.18, bf16[1024,7168]{1,0:T(8,128)(2,1)} %param.4), kind=kOutput, calls=%fused_computation.12 | convolution fusion | flops 22572169216 | bytes 72357888 | tf_op jit(solution)/shard_map/dot_general | solution.py:18
  146.3 63.2 %pmax.7 = f32[1536]{0:T(1024)S(1)} all-reduce(f32[1536]{0:T(1024)S(1)} %get-tuple-element.9), channel_id=1, replica_groups=mesh['vocab'=32,'batch'=4] {'vocab'}, use_global_device_ids=true, to_apply=%region_1.0 | all-reduce | flops 1536 | bytes 12288 | tf_op jit(solution)/shard_map/pmax | solution.py:30
  209.5 6.0 %fusion.3 = (f32[1536]{0:T(1024)S(1)}, f32[1536]{0:T(1024)S(1)}, bf16[1536,1024]{0,1:T(8,128)(2,1)}) fusion(f32[1024,1536]{1,0:T(8,128)} %get-tuple-element.10, f32[1536]{0:T(1024)S(1)} %get-tuple-element.9), kind=kLoop, calls=%fused_computation.6 | loop fusion | flops 7861248 | bytes 9455616 | tf_op jit(solution)/shard_map/reduce_sum | solution.py:28
  215.5 121.6 %all-reduce = (f32[1536]{0:T(1024)S(1)}, f32[1536]{0:T(1024)S(1)}) all-reduce(f32[1536]{0:T(1024)S(1)} %get-tuple-element.8, f32[1536]{0:T(1024)S(1)} %get-tuple-element.7), channel_id=1, replica_groups=mesh['vocab'=32,'batch'=4] {'vocab'}, use_global_device_ids=true, to_apply=%region_3.0 | all-reduce | flops 3072 | bytes 24576 | tf_op jit(solution)/shard_map/psum | solution.py:32
  337.2 2.5 multiply_convert_fusion
  339.6 2.9 copy.7
  342.5 9.4 %all-to-all-start = ((bf16[32,48,1024]{2,1,0:T(8,128)(2,1)}), bf16[32,48,1024]{2,1,0:T(8,128)(2,1)S(1)}, u32[]{:S(2)}, u32[]{:S(2)}) async-start(bf16[32,48,1024]{2,1,0:T(8,128)(2,1)} %bitcast.20), calls=%async_computation | async-start | bytes 6291456 | tf_op jit(solution)/shard_map/all_to_all | solution.py:36
  351.9 0.6 divide_subtract_fusion
  352.5 38.7 %all-to-all-done = bf16[32,48,1024]{2,1,0:T(8,128)(2,1)S(1)} async-done(((bf16[32,48,1024]{2,1,0:T(8,128)(2,1)}), bf16[32,48,1024]{2,1,0:T(8,128)(2,1)S(1)}, u32[]{:S(2)}, u32[]{:S(2)}) %all-to-all-start) | async-done | bytes 3145760 | tf_op jit(solution)/shard_map/all_to_all | solution.py:36
  391.1 2.1 copy.9
  (2 shorter events, 0.0 us)
Async XLA Ops:
  7.2 91.6 %all-gather.2.cloned.1.call-start = ((), (), s32[]{:S(2)}) async-start(), calls=%async_computation.1 | async-start | bytes 22708224 | tf_op jit(solution)/shard_map/all_gather | solution.py:19
  342.5 48.6 %all-to-all-start = ((bf16[32,48,1024]{2,1,0:T(8,128)(2,1)}), bf16[32,48,1024]{2,1,0:T(8,128)(2,1)S(1)}, u32[]{:S(2)}, u32[]{:S(2)}) async-start(bf16[32,48,1024]{2,1,0:T(8,128)(2,1)} %bitcast.20), calls=%async_computation | async-start | bytes 6291456 | tf_op jit(solution)/shard_map/all_to_all | solution.py:36
Sparse Core Ops, SparseCore 0:
  10.2 88.5 all-gather.1
where the time goes:
time: 402 us; the launch traced here: 400 us
  blocking collectives  185 us (46%)
  waiting for transfers between devices  130 us (32%)
  matrix products  35.2 us (9%)
  local copies, waits for them, and re-layouts  17.3 us (4%)
  between operations  14.1 us (4%)
  starting transfers between devices  9.41 us (2%)
  other arithmetic  9.08 us (2%)
    psum x1, blocking collectives, shards(): lax.psum((local_sum * factor, factor * (local_tilt + local_sum * (local_t...  122 us
    all_gather x1, waiting for transfers between devices, shards(): lax.all_gather(hidden, 'vocab', axis=0, tiled=True)  90.9 us
    pmax x1, blocking collectives, shards(): top_value = lax.pmax(local_top, 'vocab')  63.2 us
    all_to_all x1, waiting for transfers between devices, shards(): lax.all_to_all(spread, 'vocab', split_axis=0, concat_axis=1, tiled=True)  38.7 us
    dot_general x1, matrix products, shards(): lax.dot_general(lax.all_gather(hidden, 'vocab', axis=0, tiled=True), weig...  35.2 us
    mul x1, local copies, waits for them, and re-layouts, shards(): grouped * head_scales[:, None, :, None]  12.3 us
    all_to_all x1, starting transfers between devices, shards(): lax.all_to_all(spread, 'vocab', split_axis=0, concat_axis=1, tiled=True)  9.37 us
  transfers between devices with their start and end apart: 2, of which 2 were waited for; matrix products, arithmetic and copies ran while one was open for 0% of the time, Pallas kernels for 0%

commit v1 on v0

v1 whole, which is shorter than its diff:
```python
import functools

import jax
import jax.numpy as jnp
from jax import lax
from jax.experimental import pallas as pl
from jax.experimental.pallas import tpu as pltpu
from jax.sharding import PartitionSpec as P

MESH = pl.DeviceIdType.MESH
BLOCK = 128
TILE = 256

SLOTS = [
    (0, 0), (0, 1), (0, 3), (1, 0), (3, 0), (1, 3), (3, 1), (1, 1), (3, 3),
    (0, 2), (2, 0), (1, 2), (3, 2), (2, 1), (2, 3), (2, 2),
]
SLOT = {chip: slot for slot, chip in enumerate(SLOTS)}
UP, DOWN = 1, 3


def axis_move(half, stage, step):
    along_y = (half == 0) == (stage == 0)
    return (0, step) if along_y else (step, 0)


def add(a, b):
    return ((a[0] + b[0]) % 4, (a[1] + b[1]) % 4)


def neg(a):
    return ((-a[0]) % 4, (-a[1]) % 4)


def piece_table():
    pieces = []
    for half in (0, 1):
        for chip in SLOTS[1:]:
            first, second = (chip[1], chip[0]) if half == 0 else (chip[0], chip[1])
            last = second if second else first
            pieces += [(half, chip, q) for q in ((0, 1) if last == 2 else (None,))]
    return {piece: i for i, piece in enumerate(pieces)}


PIECE = piece_table()


def head_kernel(
    rows, hidden, codes, scales, raw, stats_in,
    gathered, weight, staged, logits, expo, stats_out,
    copy_sem, stage_sem, ici_send, ici_recv, sib_send, sib_recv, out_send, out_recv, st_send, st_recv,
):
    width = hidden.shape[1]
    vocab = codes.shape[0]
    half_w, quarter_w = width // 2, width // 4
    me = lax.axis_index("vocab")
    z, y, c = me // 8, lax.rem(me // 2, 4), lax.rem(me, 2)

    def device(chip, core=0):
        index = (lax.rem(z + chip[0], 4) * 4 + lax.rem(y + chip[1], 4)) * 2 + lax.rem(c + core, 2)
        return {"vocab": index}

    def row_block(chip, core=0):
        return pl.ds(SLOT[chip] * 2 * rows + core * rows, rows)

    def columns(half, quarter=None):
        if quarter is None:
            return pl.ds(half * half_w, half_w)
        return pl.ds(half * half_w + quarter * quarter_w, quarter_w)

    def remote(src, dst, send, recv, target):
        pltpu.make_async_remote_copy(
            src_ref=src, dst_ref=dst, send_sem=send, recv_sem=recv, device_id=target, device_id_type=MESH
        ).start()

    def pass_on(half, chip, quarter, move):
        cols = columns(half, quarter)
        there = add(chip, neg(move))
        src = hidden.at[:, cols] if chip == (0, 0) else gathered.at[row_block(chip), cols]
        remote(
            src,
            gathered.at[row_block(there), cols],
            ici_send,
            ici_recv.at[PIECE[half, there, quarter]],
            device(move),
        )

    def arrived(half, chip, quarter=None):
        cols = columns(half, quarter)
        ref = gathered.at[row_block(chip), cols]
        pltpu.make_async_copy(ref, ref, ici_recv.at[PIECE[half, chip, quarter]]).wait()

    def share(half, chip):
        cols = columns(half)
        remote(
            gathered.at[row_block(chip), cols],
            gathered.at[row_block(chip, 1), cols],
            sib_send,
            sib_recv.at[SLOT[chip] * 2 + half],
            device((0, 0), 1),
        )

    def first_pair(half):
        up, down = axis_move(half, 0, UP), axis_move(half, 0, DOWN)
        arrived(half, up)
        arrived(half, down)
        pass_on(half, up, 1, down)
        pass_on(half, down, 0, up)
        up2, down2 = axis_move(half, 1, UP), axis_move(half, 1, DOWN)
        pass_on(half, up, None, up2)
        pass_on(half, down, None, down2)
        pass_on(half, up, None, down2)
        pass_on(half, down, None, up2)
        share(half, up)
        share(half, down)

    def first_opposite(half):
        chip = axis_move(half, 0, 2)
        arrived(half, chip, 0)
        arrived(half, chip, 1)
        pass_on(half, chip, None, axis_move(half, 1, UP))
        pass_on(half, chip, None, axis_move(half, 1, DOWN))
        share(half, chip)

    def second(half, first_step, direction):
        back = axis_move(half, 1, UP if direction == DOWN else DOWN)
        chip = add(axis_move(half, 0, first_step), axis_move(half, 1, direction))
        arrived(half, chip)
        pass_on(half, chip, 1 if direction == UP else 0, back)
        share(half, chip)

    def second_opposite(half, first_step):
        chip = add(axis_move(half, 0, first_step), axis_move(half, 1, 2))
        arrived(half, chip, 0)
        arrived(half, chip, 1)
        share(half, chip)

    barrier = pltpu.get_barrier_semaphore()
    neighbours = [device((0, UP)), device((0, DOWN)), device((UP, 0)), device((DOWN, 0)), device((0, 0), 1)]
    for neighbour in neighbours:
        pl.semaphore_signal(barrier, inc=1, device_id=neighbour, device_id_type=MESH)
    pl.semaphore_wait(barrier, len(neighbours))

    own = (0, 0)
    for stage in (0, 1):
        for half in (0, 1):
            for step in (UP, DOWN):
                pass_on(half, own, None, axis_move(half, stage, step))
    own_rows = gathered.at[row_block(own), :]
    remote(hidden, gathered.at[row_block(own, 1), :], sib_send, sib_recv.at[0], device(own, 1))
    own_copy = pltpu.make_async_copy(hidden, own_rows, copy_sem)
    own_copy.start()

    def stage_in(block):
        return pltpu.make_async_copy(
            codes.at[pl.ds(block * BLOCK, BLOCK), :], staged.at[block % 2], stage_sem.at[block % 2]
        )

    def dequantize(block):
        stage_in(block).wait()

        def body(i, carry):
            for j in range(4):
                d = i * 4 + j
                at = pl.ds(pl.multiple_of(d * BLOCK, BLOCK), BLOCK)
                tile = staged[block % 2, :, at].astype(jnp.float32) * scales[block, d]
                weight[at, pl.ds(block * BLOCK, BLOCK)] = tile.astype(jnp.bfloat16).T
            return carry

        lax.fori_loop(0, width // (4 * BLOCK), body, 0)
        if block + 2 < vocab // BLOCK:
            stage_in(block + 2).start()

    lane = lax.broadcasted_iota(jnp.int32, (rows, 128), 1)

    def compute(chips):
        base = SLOT[chips[0]] * 2 * rows
        count = len(chips) * 2 * rows
        for chip in chips:
            for half in (0, 1):
                if chip == own and half:
                    continue
                ref = gathered.at[row_block(chip, 1), pl.ds(0, width) if chip == own else columns(half)]
                pltpu.make_async_copy(ref, ref, sib_recv.at[SLOT[chip] * 2 + half]).wait()

        def body(i, carry):
            at = pl.ds(pl.multiple_of(i * TILE, TILE), TILE)
            logits[0:count, at] = jnp.dot(
                gathered[base : base + count, :], weight[:, at], preferred_element_type=jnp.float32
            )
            return carry

        lax.fori_loop(0, vocab // TILE, body, 0)
        for core in (0, 1):
            for i, chip in enumerate(chips):
                part = i * 2 + core
                value = logits[part * rows : (part + 1) * rows, :]
                top = jnp.max(value, axis=1, keepdims=True)
                shift = value - top
                expf = jnp.exp(shift)
                total = jnp.sum(expf, axis=1, keepdims=True)
                tilt = jnp.sum(expf * shift, axis=1, keepdims=True)
                at = row_block(chip, core)
                expo[at, :] = expf.astype(jnp.bfloat16)
                packed = jnp.where(lane == 0, top, jnp.where(lane == 1, total, tilt))
                packed = jnp.concatenate([packed, jnp.zeros((128 - rows, 128), jnp.float32)], axis=0)
                index = SLOT[chip] * 2 + core
                stats_out[index] = packed.T[0:8, :]
                there = raw.at[:, pl.ds(pl.multiple_of(me * vocab, vocab), vocab)]
                if chip == own and core == 0:
                    pltpu.make_async_copy(expo.at[at, :], there, out_recv).start()
                    pltpu.make_async_copy(stats_out.at[index], stats_in.at[me], st_recv).start()
                else:
                    remote(expo.at[at, :], there, out_send, out_recv, device(chip, core))
                    remote(stats_out.at[index], stats_in.at[me], st_send, st_recv, device(chip, core))

    stage_in(0).start()
    stage_in(1).start()
    for block in range(vocab // BLOCK):
        dequantize(block)
        if block == 3:
            first_pair(0)
            first_pair(1)
    for half in (0, 1):
        second(half, 0, UP)
        second(half, 0, DOWN)
    own_copy.wait()
    compute([own])
    first_opposite(0)
    first_opposite(1)
    compute([(0, 1), (0, 3)])
    for half in (0, 1):
        second(half, UP, DOWN)
        second(half, DOWN, UP)
    compute([(1, 0), (3, 0)])
    compute([(1, 3), (3, 1)])
    for half in (0, 1):
        second(half, UP, UP)
        second(half, DOWN, DOWN)
    compute([(1, 1), (3, 3)])
    second_opposite(0, 0)
    second_opposite(1, 0)
    compute([(0, 2), (2, 0)])
    for half in (0, 1):
        second(half, 2, UP)
        second(half, 2, DOWN)
    for half in (0, 1):
        second_opposite(half, UP)
        second_opposite(half, DOWN)
    compute([(1, 2), (3, 2)])
    compute([(2, 1), (2, 3)])
    second_opposite(0, 2)
    second_opposite(1, 2)
    compute([(2, 2)])

    def wait_bytes(ref, sem):
        pltpu.make_async_copy(ref, ref, sem).wait()

    wait_bytes(gathered.at[pl.ds(0, 15 * rows), :], ici_send)
    wait_bytes(gathered.at[pl.ds(0, 16 * rows), :], sib_send)
    wait_bytes(expo.at[pl.ds(0, 31 * rows), :], out_send)
    wait_bytes(stats_out.at[pl.ds(0, 31)], st_send)
    wait_bytes(raw, out_recv)
    wait_bytes(stats_in, st_recv)


def scale_kernel(rows, stats, raw, out, entropy, scale):
    blocks = stats.shape[0]
    step = pl.program_id(0)
    vocab = raw.shape[1] * pl.num_programs(0) // blocks
    per_step = raw.shape[1] // vocab

    @pl.when(step == 0)
    def _():
        top, total, tilt = stats[:, 0, :], stats[:, 1, :], stats[:, 2, :]
        top_value = jnp.max(top, axis=0, keepdims=True)
        factor = jnp.exp(top - top_value)
        exp_sum = jnp.sum(total * factor, axis=0, keepdims=True)
        tilt_sum = jnp.sum(factor * (tilt + total * (top - top_value)), axis=0, keepdims=True)
        entropy[...] = jnp.log(exp_sum) - tilt_sum / exp_sum
        ratio = factor / exp_sum
        ratio = jnp.concatenate([ratio, jnp.zeros((128 - blocks, 128), jnp.float32)], axis=0).T
        for s in range(blocks // per_step):
            scale[s] = ratio[0:rows, s * per_step : (s + 1) * per_step]

    ratio = scale[step]
    for b in range(per_step):
        at = slice(b * vocab, (b + 1) * vocab)
        out[:, at] = (raw[:, at].astype(jnp.float32) * ratio[:, b : b + 1]).astype(jnp.bfloat16)


def shards(n_vocab, hidden, head_codes, head_scales):
    rows, width = hidden.shape
    vocab = head_codes.shape[0]
    hbm, smem = pl.BlockSpec(memory_space=pl.ANY), pl.BlockSpec(memory_space=pltpu.SMEM)
    dma = pltpu.SemaphoreType.DMA
    raw, stats = pl.pallas_call(
        functools.partial(head_kernel, rows),
        out_shape=(
            jax.ShapeDtypeStruct((rows, n_vocab * vocab), jnp.bfloat16),
            jax.ShapeDtypeStruct((n_vocab, 8, 128), jnp.float32),
        ),
        in_specs=[hbm, hbm, smem],
        out_specs=(hbm, hbm),
        scratch_shapes=[
            pltpu.VMEM((n_vocab * rows, width), jnp.bfloat16),
            pltpu.VMEM((width, vocab), jnp.bfloat16),
            pltpu.VMEM((2, BLOCK, width), jnp.bfloat16),
            pltpu.VMEM((4 * rows, vocab), jnp.float32),
            pltpu.VMEM((n_vocab * rows, vocab), jnp.bfloat16),
            pltpu.VMEM((n_vocab, 8, 128), jnp.float32),
            dma, dma((2,)), dma, dma((len(PIECE),)), dma, dma((32,)), dma, dma, dma, dma,
        ],
        compiler_params=pltpu.CompilerParams(
            collective_id=0, has_side_effects=True, vmem_limit_bytes=60 << 20
        ),
        cost_estimate=pl.CostEstimate(
            flops=2 * n_vocab * rows * width * vocab,
            bytes_accessed=2 * vocab * width,
            transcendentals=n_vocab * rows * vocab,
        ),
        name="head",
    )(hidden, head_codes, head_scales)
    steps = 4
    cut = n_vocab * vocab // steps
    probabilities, entropy = pl.pallas_call(
        functools.partial(scale_kernel, rows),
        grid=(steps,),
        out_shape=(
            jax.ShapeDtypeStruct((rows, n_vocab * vocab), jnp.bfloat16),
            jax.ShapeDtypeStruct((1, 128), jnp.float32),
        ),
        in_specs=[
            pl.BlockSpec((n_vocab, 8, 128), lambda i: (0, 0, 0)),
            pl.BlockSpec((rows, cut), lambda i: (0, i)),
        ],
        out_specs=(pl.BlockSpec((rows, cut), lambda i: (0, i)), pl.BlockSpec((1, 128), lambda i: (0, 0))),
        scratch_shapes=[pltpu.VMEM((steps, rows, n_vocab // steps), jnp.float32)],
        compiler_params=pltpu.CompilerParams(vmem_limit_bytes=32 << 20),
        name="scale",
    )(stats, raw)
    return probabilities, entropy[0, :rows]


def solution(mesh):
    placed = P(("batch", "vocab"), None)
    return jax.shard_map(
        functools.partial(shards, mesh.shape["vocab"]),
        mesh=mesh,
        in_specs=(placed, placed, placed),
        out_specs=(placed, P(("batch", "vocab"))),
        check_vma=False,
    )
```

time: 402 us -> 112 us (0.28)
  blocking collectives: 185 us -> 0 us
  waiting for transfers between devices: 130 us -> 0 us
  Pallas kernels: 0 us -> 107 us
  matrix products: 35.2 us -> 0 us
  local copies, waits for them, and re-layouts: 17.3 us -> 3.3 us
  between operations: 14.1 us -> 0.65 us
  starting transfers between devices: 9.41 us -> 0 us
  other arithmetic: 9.08 us -> 0 us
    psum x1 -> x0, blocking collectives: 122 us -> none  [shards(): lax.psum((local_sum * factor, factor * (local_tilt + local_sum * (local_t...]
    pallas_call x0 -> x2, Pallas kernels: none -> 107 us  [the longest x1 105 us: shards(): pl.pallas_call(functools.partial(head_kernel, rows), out_shape=(jax.Shape...]
    all_gather x1 -> x0, waiting for transfers between devices: 90.9 us -> none  [shards(): lax.all_gather(hidden, 'vocab', axis=0, tiled=True)]
    pmax x1 -> x0, blocking collectives: 63.2 us -> none  [shards(): top_value = lax.pmax(local_top, 'vocab')]
    all_to_all x1 -> x0, waiting for transfers between devices: 38.7 us -> none  [shards(): lax.all_to_all(spread, 'vocab', split_axis=0, concat_axis=1, tiled=True)]
    dot_general x1 -> x0, matrix products: 35.2 us -> none  [shards(): lax.dot_general(lax.all_gather(hidden, 'vocab', axis=0, tiled=True), weig...]
    mul x1 -> x0, local copies, waits for them, and re-layouts: 12.3 us -> none  [shards(): grouped * head_scales[:, None, :, None]]
    all_to_all x1 -> x0, starting transfers between devices: 9.37 us -> none  [shards(): lax.all_to_all(spread, 'vocab', split_axis=0, concat_axis=1, tiled=True)]
  transfers between devices with their start and end apart: 2 -> 0, of which waited for: 2 -> 0; matrix products, arithmetic and copies ran while one was open for 0% -> 0% of each run, Pallas kernels for 0% -> 0%
where the time goes in v1:
time: 112 us; the launch traced here: 111 us
  Pallas kernels  107 us (96%)
  local copies, waits for them, and re-layouts  3.3 us (3%)
    pallas_call x1, Pallas kernels, shards(): pl.pallas_call(functools.partial(head_kernel, rows), out_shape=(jax.Shape...  105 us
    pallas_call x1, Pallas kernels, shards(): pl.pallas_call(functools.partial(scale_kernel, rows), grid=(steps,), out_...  2.8 us
    unnamed x4, local copies, waits for them, and re-layouts  2.79 us

profile of v1, /device:TPU:1, one launch (start us, length us, event | category | flops | bytes accessed | tf_op | source)
XLA Modules:
  0.0 111.4 jit_solution(15410924973501287434)
XLA Ops:
  0.6 104.6 %head.1 = (bf16[48,32768]{1,0:T(8,128)(2,1)}, f32[32,8,128]{2,1,0:T(8,128)}) custom-call(bf16[48,7168]{1,0:T(8,128)(2,1)} %hidden.1, bf16[1024,7168]{1,0:T(8,128)(2,1)} %codes.1, f32[8,56]{1,0:T(8,128)} %scales.1), custom_call_target="tpu_custom_call" | custom-call | flops 22548578304 | bytes 14680064 | tf_op jit(solution)/shard_map/head/pallas_call | solution.py:297
  105.2 0.0 copy-start
  105.3 1.9 %copy-done = bf16[48,32768]{1,0:T(8,128)(2,1)S(1)} copy-done((bf16[48,32768]{1,0:T(8,128)(2,1)S(1)}, bf16[48,32768]{1,0:T(8,128)(2,1)}, u32[]{:S(2)}) %copy-start) | copy-done | bytes 3145752
  107.1 0.0 copy-start.1
  107.1 0.9 copy-done.1
  108.0 2.8 %scale.1 = (bf16[48,32768]{1,0:T(8,128)(2,1)}, f32[1,128]{1,0:T(1,128)S(1)}) custom-call(f32[32,8,128]{2,1,0:T(8,128)S(1)} %copy-done.1, bf16[48,32768]{1,0:T(8,128)(2,1)S(1)} %copy-done), custom_call_target="tpu_custom_call" | custom-call | tf_op jit(solution)/shard_map/scale/pallas_call | solution.py:326
  110.8 0.5 slice_bitcast_fusion
Async XLA Ops:
  105.2 1.9 %copy-start = (bf16[48,32768]{1,0:T(8,128)(2,1)S(1)}, bf16[48,32768]{1,0:T(8,128)(2,1)}, u32[]{:S(2)}) copy-start(bf16[48,32768]{1,0:T(8,128)(2,1)} %get-tuple-element.7.raw) | copy-start | bytes 9437188
  107.1 0.9 copy-start.1

commit v2 on v1

v2 whole, which is shorter than its diff:
```python
import functools

import jax
import jax.numpy as jnp
from jax import lax
from jax.experimental import pallas as pl
from jax.experimental.pallas import tpu as pltpu
from jax.sharding import PartitionSpec as P

MESH = pl.DeviceIdType.MESH
BLOCK = 128
TILE = 256

STEPS = [
    [(0, 0)], [(0, 1), (0, 3)], [(1, 0), (3, 0)], [(1, 3), (3, 1)], [(1, 1), (3, 3)],
    [(0, 2), (2, 0)], [(1, 2), (2, 1)], [(3, 2), (2, 3)], [(2, 2)],
]
SLOTS = [chip for chips in STEPS for chip in chips]
SLOT = {chip: slot for slot, chip in enumerate(SLOTS)}
def add(a, b):
    return ((a[0] + b[0]) % 4, (a[1] + b[1]) % 4)


def neg(a):
    return ((-a[0]) % 4, (-a[1]) % 4)


def link_sends(along_y, step):
    first, second = (0, 1) if along_y else (1, 0)
    quarter = 0 if step == 1 else 1

    def chip(other, this):
        return (other % 4, this % 4) if along_y else (this % 4, other % 4)

    return [
        (first, chip(0, 0), None),
        (second, chip(0, 0), None),
        (first, chip(0, -step), quarter),
        (second, chip(step, 0), None),
        (second, chip(-step, 0), None),
        (second, chip(0, -step), quarter),
        (second, chip(2, 0), None),
        (second, chip(1, -step), quarter),
        (second, chip(-1, -step), quarter),
        (second, chip(2, -step), quarter),
    ]


LINKS = [(move, link_sends(move[0] == 0, sum(move))) for move in ((0, 1), (0, -1), (1, 0), (-1, 0))]
ROUNDS = 10
AHEAD = 3

def head_kernel(
    rows, hidden, codes, scales_in, raw, stats_in,
    scales, gathered, weight, staged, logits, expo, stats_out,
    scale_sem, copy_sem, stage_sem, ici_send, ici_recv, sib_send, sib_recv, out_send, out_recv, st_send, st_recv,
):
    width = hidden.shape[1]
    vocab = codes.shape[0]
    half_w, quarter_w = width // 2, width // 4
    me = lax.axis_index("vocab")
    z, y, c = me // 8, lax.rem(me // 2, 4), lax.rem(me, 2)

    def device(chip, core=0):
        index = (lax.rem(z + chip[0] % 4, 4) * 4 + lax.rem(y + chip[1] % 4, 4)) * 2 + lax.rem(c + core, 2)
        return {"vocab": index}

    def row_block(chip, core=0):
        return pl.ds(SLOT[chip] * 2 * rows + core * rows, rows)

    def columns(half, quarter=None):
        if quarter is None:
            return pl.ds(half * half_w, half_w)
        return pl.ds(half * half_w + quarter * quarter_w, quarter_w)

    def remote(src, dst, send, recv, target):
        pltpu.make_async_remote_copy(
            src_ref=src, dst_ref=dst, send_sem=send, recv_sem=recv, device_id=target, device_id_type=MESH
        ).start()

    def send(turn):
        for link, (move, sends) in enumerate(LINKS):
            half, chip, quarter = sends[turn]
            cols = columns(half, quarter)
            src = hidden.at[:, cols] if chip == (0, 0) else gathered.at[row_block(chip), cols]
            dst = gathered.at[row_block(add(chip, neg(move))), cols]
            remote(src, dst, ici_send, ici_recv.at[link * ROUNDS + turn], device(move))

    def receive(turn):
        halves = []
        for link, (move, sends) in enumerate(LINKS):
            half, chip, quarter = sends[turn]
            chip = add(chip, neg(move))
            ref = gathered.at[row_block(chip), columns(half, quarter)]
            pltpu.make_async_copy(ref, ref, ici_recv.at[link * ROUNDS + turn]).wait()
            if (half, chip) not in halves:
                halves.append((half, chip))
        if turn == 0:
            for early in range(2, AHEAD):
                send(early)
        if turn + AHEAD < ROUNDS:
            send(turn + AHEAD)
        for half, chip in halves:
            at = columns(half)
            remote(
                gathered.at[row_block(chip), at],
                gathered.at[row_block(chip, 1), at],
                sib_send,
                sib_recv.at[SLOT[chip] * 2 + half],
                device((0, 0), 1),
            )

    scale_copy = pltpu.make_async_copy(scales_in, scales, scale_sem)
    scale_copy.start()

    barrier = pltpu.get_barrier_semaphore()
    neighbours = [device(move) for move, _ in LINKS] + [device((0, 0), 1)]
    for neighbour in neighbours:
        pl.semaphore_signal(barrier, inc=1, device_id=neighbour, device_id_type=MESH)
    pl.semaphore_wait(barrier, len(neighbours))

    own = (0, 0)
    send(0)
    send(1)
    own_rows = gathered.at[row_block(own), :]
    remote(hidden, gathered.at[row_block(own, 1), :], sib_send, sib_recv.at[0], device(own, 1))
    own_copy = pltpu.make_async_copy(hidden, own_rows, copy_sem)
    own_copy.start()

    def stage_in(block):
        return pltpu.make_async_copy(
            codes.at[pl.ds(block * BLOCK, BLOCK), :], staged.at[block % 2], stage_sem.at[block % 2]
        )

    def dequantize(block):
        stage_in(block).wait()

        def body(i, carry):
            for j in range(4):
                d = i * 4 + j
                at = pl.ds(pl.multiple_of(d * BLOCK, BLOCK), BLOCK)
                tile = staged[block % 2, :, at].astype(jnp.float32) * scales[block, d]
                weight[at, pl.ds(block * BLOCK, BLOCK)] = tile.astype(jnp.bfloat16).T
            return carry

        lax.fori_loop(0, width // (4 * BLOCK), body, 0)
        if block + 2 < vocab // BLOCK:
            stage_in(block + 2).start()

    lane = lax.broadcasted_iota(jnp.int32, (rows, 128), 1)

    def compute(chips):
        base = SLOT[chips[0]] * 2 * rows
        count = len(chips) * 2 * rows
        for chip in chips:
            for half in (0, 1):
                if chip == own and half:
                    continue
                ref = gathered.at[row_block(chip, 1), pl.ds(0, width) if chip == own else columns(half)]
                pltpu.make_async_copy(ref, ref, sib_recv.at[SLOT[chip] * 2 + half]).wait()

        def body(i, carry):
            at = pl.ds(pl.multiple_of(i * TILE, TILE), TILE)
            logits[0:count, at] = jnp.dot(
                gathered[base : base + count, :], weight[:, at], preferred_element_type=jnp.float32
            )
            return carry

        lax.fori_loop(0, vocab // TILE, body, 0)
        for core in (0, 1):
            for i, chip in enumerate(chips):
                part = i * 2 + core
                value = logits[part * rows : (part + 1) * rows, :]
                top = jnp.max(value, axis=1, keepdims=True)
                shift = value - top
                expf = jnp.exp(shift)
                total = jnp.sum(expf, axis=1, keepdims=True)
                tilt = jnp.sum(expf * shift, axis=1, keepdims=True)
                at = row_block(chip, core)
                expo[at, :] = expf.astype(jnp.bfloat16)
                packed = jnp.where(lane == 0, top, jnp.where(lane == 1, total, tilt))
                packed = jnp.concatenate([packed, jnp.zeros((128 - rows, 128), jnp.float32)], axis=0)
                index = SLOT[chip] * 2 + core
                turned = packed.T
                for k in range(3):
                    stats_out[index, :, k * 128 : (k + 1) * 128] = turned[k : k + 1, :]
                there = raw.at[:, pl.ds(pl.multiple_of(me * vocab, vocab), vocab)]
                if chip == own and core == 0:
                    pltpu.make_async_copy(expo.at[at, :], there, out_recv).start()
                    pltpu.make_async_copy(stats_out.at[index], stats_in.at[me], st_recv).start()
                else:
                    remote(expo.at[at, :], there, out_send, out_recv, device(chip, core))
                    remote(stats_out.at[index], stats_in.at[me], st_send, st_recv, device(chip, core))

    stage_in(0).start()
    stage_in(1).start()
    scale_copy.wait()
    for block in range(vocab // BLOCK):
        dequantize(block)
        if block == 3:
            receive(0)
    receive(1)
    own_copy.wait()
    compute(STEPS[0])
    compute(STEPS[1])
    receive(2)
    compute(STEPS[2])
    receive(3)
    compute(STEPS[3])
    receive(4)
    compute(STEPS[4])
    receive(5)
    compute(STEPS[5])
    receive(6)
    receive(7)
    compute(STEPS[6])
    receive(8)
    compute(STEPS[7])
    receive(9)
    compute(STEPS[8])

    def wait_bytes(ref, sem):
        pltpu.make_async_copy(ref, ref, sem).wait()

    wait_bytes(gathered.at[pl.ds(0, 15 * rows), :], ici_send)
    wait_bytes(gathered.at[pl.ds(0, 16 * rows), :], sib_send)
    wait_bytes(expo.at[pl.ds(0, 31 * rows), :], out_send)
    wait_bytes(stats_out.at[pl.ds(0, 31)], st_send)
    wait_bytes(raw, out_recv)
    wait_bytes(stats_in, st_recv)


def scale_kernel(rows, per_step, stats, raw, out, entropy, ready, sems):
    blocks = stats.shape[0]
    vocab = raw.shape[1] // blocks
    top, total, tilt = stats[:, 0, 0:128], stats[:, 0, 128:256], stats[:, 0, 256:384]
    top_value = jnp.max(top, axis=0, keepdims=True)
    factor = jnp.exp(top - top_value)
    exp_sum = jnp.sum(total * factor, axis=0, keepdims=True)
    tilt_sum = jnp.sum(factor * (tilt + total * (top - top_value)), axis=0, keepdims=True)
    entropy[...] = (jnp.log(exp_sum) - tilt_sum / exp_sum)[0, 0:rows]
    ratio = factor / exp_sum
    ratio = jnp.concatenate([ratio, jnp.zeros((128 - blocks, 128), jnp.float32)], axis=0).T[0:rows]
    copies = []
    for step in range(blocks // per_step):
        cols = pl.ds(step * per_step * vocab, per_step * vocab)
        for b in range(step * per_step, (step + 1) * per_step):
            at = slice(b * vocab, (b + 1) * vocab)
            ready[:, at] = (raw[:, at].astype(jnp.float32) * ratio[:, b : b + 1]).astype(jnp.bfloat16)
        copies.append(pltpu.make_async_copy(ready.at[:, cols], out.at[:, cols], sems.at[step]))
        copies[-1].start()
    for copy in copies:
        copy.wait()


def shards(n_vocab, hidden, head_codes, head_scales):
    rows, width = hidden.shape
    vocab = head_codes.shape[0]
    hbm = pl.BlockSpec(memory_space=pltpu.HBM)
    vmem = pl.BlockSpec(memory_space=pltpu.VMEM)
    dma = pltpu.SemaphoreType.DMA
    raw, stats = pl.pallas_call(
        functools.partial(head_kernel, rows),
        out_shape=(
            jax.ShapeDtypeStruct((rows, n_vocab * vocab), jnp.bfloat16),
            jax.ShapeDtypeStruct((n_vocab, 1, 384), jnp.float32),
        ),
        in_specs=[hbm, hbm, hbm],
        out_specs=(vmem, vmem),
        scratch_shapes=[
            pltpu.SMEM(head_scales.shape, jnp.float32),
            pltpu.VMEM((n_vocab * rows, width), jnp.bfloat16),
            pltpu.VMEM((width, vocab), jnp.bfloat16),
            pltpu.VMEM((2, BLOCK, width), jnp.bfloat16),
            pltpu.VMEM((4 * rows, vocab), jnp.float32),
            pltpu.VMEM((n_vocab * rows, vocab), jnp.bfloat16),
            pltpu.VMEM((n_vocab, 1, 384), jnp.float32),
            dma, dma, dma((2,)), dma, dma((len(LINKS) * ROUNDS,)), dma, dma((32,)), dma, dma, dma, dma,
        ],
        compiler_params=pltpu.CompilerParams(
            collective_id=0, has_side_effects=True, vmem_limit_bytes=50 << 20
        ),
        cost_estimate=pl.CostEstimate(
            flops=2 * n_vocab * rows * width * vocab,
            bytes_accessed=2 * vocab * width,
            transcendentals=n_vocab * rows * vocab,
        ),
        name="head",
    )(*(pltpu.with_memory_space_constraint(x, pltpu.HBM) for x in (hidden, head_codes, head_scales)))
    steps = 8
    probabilities, entropy = pl.pallas_call(
        functools.partial(scale_kernel, rows, n_vocab // steps),
        out_shape=(
            jax.ShapeDtypeStruct((rows, n_vocab * vocab), jnp.bfloat16),
            jax.ShapeDtypeStruct((rows,), jnp.float32),
        ),
        in_specs=[vmem, vmem],
        out_specs=(hbm, vmem),
        scratch_shapes=[pltpu.VMEM((rows, n_vocab * vocab), jnp.bfloat16), dma((steps,))],
        compiler_params=pltpu.CompilerParams(vmem_limit_bytes=16 << 20),
        name="scale",
    )(stats, raw)
    return probabilities, entropy


def solution(mesh):
    placed = P(("batch", "vocab"), None)
    return jax.shard_map(
        functools.partial(shards, mesh.shape["vocab"]),
        mesh=mesh,
        in_specs=(placed, placed, placed),
        out_specs=(placed, P(("batch", "vocab"))),
        check_vma=False,
    )
```

time: 112 us -> 105 us (0.938)
  local copies, waits for them, and re-layouts: 3.3 us -> 0 us
  Pallas kernels: 107 us -> 104 us
    pallas_call x1, Pallas kernels: 105 us -> 101 us  [shards(): pl.pallas_call(functools.partial(head_kernel, rows), out_shape=(jax.Shape...]
    unnamed x4 -> x0, local copies, waits for them, and re-layouts: 2.79 us -> none
where the time goes in v2:
time: 105 us; the launch traced here: 104 us
  Pallas kernels  104 us (99%)
    pallas_call x1, Pallas kernels, shards(): pl.pallas_call(functools.partial(head_kernel, rows), out_shape=(jax.Shape...  101 us
    pallas_call x1, Pallas kernels, shards(): pl.pallas_call(functools.partial(scale_kernel, rows, n_vocab // steps), o...  2.64 us

profile of v2, /device:TPU:1, one launch (start us, length us, event | category | flops | bytes accessed | tf_op | source)
XLA Modules:
  0.0 104.5 jit_solution(2347582834308867698)
XLA Ops:
  0.6 101.2 %head.1 = (bf16[48,32768]{1,0:T(8,128)(2,1)S(1)}, f32[32,1,384]{2,1,0:T(1,128)S(1)}) custom-call(bf16[48,7168]{1,0:T(8,128)(2,1)} %hidden.1, bf16[1024,7168]{1,0:T(8,128)(2,1)} %codes.1, f32[8,56]{1,0:T(8,128)} %scales_in.1), custom_call_target="tpu_custom_call" | custom-call | flops 22548578304 | bytes 14680064 | tf_op jit(solution)/shard_map/head/pallas_call | solution.py:262
  101.8 2.6 %scale.1 = (bf16[48,32768]{1,0:T(8,128)(2,1)}, f32[48]{0:T(128)}) custom-call(f32[32,1,384]{2,1,0:T(1,128)S(1)} %get-tuple-element.4.stats, bf16[48,32768]{1,0:T(8,128)(2,1)S(1)} %get-tuple-element.5.raw), custom_call_target="tpu_custom_call" | custom-call | tf_op jit(solution)/shard_map/scale/pallas_call | solution.py:291

commit v3 on v2

--- a/solution.py
+++ b/solution.py
@@ -48,11 +48,26 @@
 
 LINKS = [(move, link_sends(move[0] == 0, sum(move))) for move in ((0, 1), (0, -1), (1, 0), (-1, 0))]
 ROUNDS = 10
-AHEAD = 3
+AHEAD = 4
+
+
+def send_turns():
+    here = {}
+    for move, sends in LINKS:
+        for turn, (half, chip, _) in enumerate(sends):
+            piece = (half, add(chip, neg(move)))
+            here[piece] = max(turn, here.get(piece, 0))
+    return [
+        [max(here.get((half, chip), -1), turn - AHEAD if turn > 1 else -1) for turn, (half, chip, _) in enumerate(sends)]
+        for _, sends in LINKS
+    ]
+
+
+SEND_TURNS = send_turns()
 
 def head_kernel(
-    rows, hidden, codes, scales_in, raw, stats_in,
-    scales, gathered, weight, staged, logits, expo, stats_out,
+    rows, hidden, codes, scales_in, raw, ratio, entropy,
+    scales, stats_in, gathered, weight, staged, logits, expo, stats_out,
     scale_sem, copy_sem, stage_sem, ici_send, ici_recv, sib_send, sib_recv, out_send, out_recv, st_send, st_recv,
 ):
     width = hidden.shape[1]
@@ -78,13 +93,16 @@
             src_ref=src, dst_ref=dst, send_sem=send, recv_sem=recv, device_id=target, device_id_type=MESH
         ).start()
 
-    def send(turn):
-        for link, (move, sends) in enumerate(LINKS):
-            half, chip, quarter = sends[turn]
-            cols = columns(half, quarter)
-            src = hidden.at[:, cols] if chip == (0, 0) else gathered.at[row_block(chip), cols]
-            dst = gathered.at[row_block(add(chip, neg(move))), cols]
-            remote(src, dst, ici_send, ici_recv.at[link * ROUNDS + turn], device(move))
+    def send(after):
+        for turn in range(ROUNDS):
+            for link, (move, sends) in enumerate(LINKS):
+                if SEND_TURNS[link][turn] != after:
+                    continue
+                half, chip, quarter = sends[turn]
+                cols = columns(half, quarter)
+                src = hidden.at[:, cols] if chip == (0, 0) else gathered.at[row_block(chip), cols]
+                dst = gathered.at[row_block(add(chip, neg(move))), cols]
+                remote(src, dst, ici_send, ici_recv.at[link * ROUNDS + turn], device(move))
 
     def receive(turn):
         halves = []
@@ -95,11 +113,7 @@
             pltpu.make_async_copy(ref, ref, ici_recv.at[link * ROUNDS + turn]).wait()
             if (half, chip) not in halves:
                 halves.append((half, chip))
-        if turn == 0:
-            for early in range(2, AHEAD):
-                send(early)
-        if turn + AHEAD < ROUNDS:
-            send(turn + AHEAD)
+        send(turn)
         for half, chip in halves:
             at = columns(half)
             remote(
@@ -120,8 +134,7 @@
     pl.semaphore_wait(barrier, len(neighbours))
 
     own = (0, 0)
-    send(0)
-    send(1)
+    send(-1)
     own_rows = gathered.at[row_block(own), :]
     remote(hidden, gathered.at[row_block(own, 1), :], sib_send, sib_recv.at[0], device(own, 1))
     own_copy = pltpu.make_async_copy(hidden, own_rows, copy_sem)
@@ -149,7 +162,23 @@
 
     lane = lax.broadcasted_iota(jnp.int32, (rows, 128), 1)
 
-    def compute(chips):
+    def deliver(chip, core):
+        index = SLOT[chip] * 2 + core
+        block, stats = expo.at[row_block(chip, core), :], stats_out.at[index]
+        there = raw.at[:, pl.ds(pl.multiple_of(me * vocab, vocab), vocab)]
+        if chip == own and core == 0:
+            pltpu.make_async_copy(block, there, out_recv).start()
+            pltpu.make_async_copy(stats, stats_in.at[me], st_recv).start()
+        else:
+            remote(stats, stats_in.at[me], st_send, st_recv, device(chip, core))
+            remote(block, there, out_send, out_recv, device(chip, core))
+
+    def deliver_all(chips):
+        for core in (0, 1):
+            for chip in chips:
+                deliver(chip, core)
+
+    def compute(chips, send_now=True):
         base = SLOT[chips[0]] * 2 * rows
         count = len(chips) * 2 * rows
         for chip in chips:
@@ -184,13 +213,8 @@
                 turned = packed.T
                 for k in range(3):
                     stats_out[index, :, k * 128 : (k + 1) * 128] = turned[k : k + 1, :]
-                there = raw.at[:, pl.ds(pl.multiple_of(me * vocab, vocab), vocab)]
-                if chip == own and core == 0:
-                    pltpu.make_async_copy(expo.at[at, :], there, out_recv).start()
-                    pltpu.make_async_copy(stats_out.at[index], stats_in.at[me], st_recv).start()
-                else:
-                    remote(expo.at[at, :], there, out_send, out_recv, device(chip, core))
-                    remote(stats_out.at[index], stats_in.at[me], st_send, st_recv, device(chip, core))
+                if send_now:
+                    deliver(chip, core)
 
     stage_in(0).start()
     stage_in(1).start()
@@ -201,10 +225,10 @@
             receive(0)
     receive(1)
     own_copy.wait()
-    compute(STEPS[0])
-    compute(STEPS[1])
+    compute(STEPS[0], False)
+    compute(STEPS[1], False)
     receive(2)
-    compute(STEPS[2])
+    compute(STEPS[2], False)
     receive(3)
     compute(STEPS[3])
     receive(4)
@@ -214,9 +238,11 @@
     receive(6)
     receive(7)
     compute(STEPS[6])
+    deliver_all([chip for pair in zip(STEPS[1], STEPS[2]) for chip in pair])
     receive(8)
     compute(STEPS[7])
     receive(9)
+    deliver_all(STEPS[0])
     compute(STEPS[8])
 
     def wait_bytes(ref, sem):
@@ -226,21 +252,22 @@
     wait_bytes(gathered.at[pl.ds(0, 16 * rows), :], sib_send)
     wait_bytes(expo.at[pl.ds(0, 31 * rows), :], out_send)
     wait_bytes(stats_out.at[pl.ds(0, 31)], st_send)
-    wait_bytes(raw, out_recv)
     wait_bytes(stats_in, st_recv)
-
-
-def scale_kernel(rows, per_step, stats, raw, out, entropy, ready, sems):
-    blocks = stats.shape[0]
-    vocab = raw.shape[1] // blocks
-    top, total, tilt = stats[:, 0, 0:128], stats[:, 0, 128:256], stats[:, 0, 256:384]
+    blocks = stats_in.shape[0]
+    top, total, tilt = (stats_in[:, 0, k * 128 : (k + 1) * 128] for k in range(3))
     top_value = jnp.max(top, axis=0, keepdims=True)
     factor = jnp.exp(top - top_value)
     exp_sum = jnp.sum(total * factor, axis=0, keepdims=True)
     tilt_sum = jnp.sum(factor * (tilt + total * (top - top_value)), axis=0, keepdims=True)
-    entropy[...] = (jnp.log(exp_sum) - tilt_sum / exp_sum)[0, 0:rows]
-    ratio = factor / exp_sum
-    ratio = jnp.concatenate([ratio, jnp.zeros((128 - blocks, 128), jnp.float32)], axis=0).T[0:rows]
+    entropy[...] = jnp.log(exp_sum) - tilt_sum / exp_sum
+    share_of_sum = jnp.concatenate([factor / exp_sum, jnp.zeros((128 - blocks, 128), jnp.float32)], axis=0)
+    ratio[...] = share_of_sum.T[0:rows]
+    wait_bytes(raw, out_recv)
+
+
+def scale_kernel(rows, per_step, blocks, entropy_in, ratio, raw, out, entropy, ready, sems):
+    vocab = raw.shape[1] // blocks
+    entropy[...] = entropy_in[0, 0:rows]
     copies = []
     for step in range(blocks // per_step):
         cols = pl.ds(step * per_step * vocab, per_step * vocab)
@@ -259,16 +286,18 @@
     hbm = pl.BlockSpec(memory_space=pltpu.HBM)
     vmem = pl.BlockSpec(memory_space=pltpu.VMEM)
     dma = pltpu.SemaphoreType.DMA
-    raw, stats = pl.pallas_call(
+    raw, ratio, entropy = pl.pallas_call(
         functools.partial(head_kernel, rows),
         out_shape=(
             jax.ShapeDtypeStruct((rows, n_vocab * vocab), jnp.bfloat16),
-            jax.ShapeDtypeStruct((n_vocab, 1, 384), jnp.float32),
+            jax.ShapeDtypeStruct((rows, 128), jnp.float32),
+            jax.ShapeDtypeStruct((1, 128), jnp.float32),
         ),
         in_specs=[hbm, hbm, hbm],
-        out_specs=(vmem, vmem),
+        out_specs=(vmem, vmem, vmem),
         scratch_shapes=[
             pltpu.SMEM(head_scales.shape, jnp.float32),
+            pltpu.VMEM((n_vocab, 1, 384), jnp.float32),
             pltpu.VMEM((n_vocab * rows, width), jnp.bfloat16),
             pltpu.VMEM((width, vocab), jnp.bfloat16),
             pltpu.VMEM((2, BLOCK, width), jnp.bfloat16),
@@ -289,17 +318,17 @@
     )(*(pltpu.with_memory_space_constraint(x, pltpu.HBM) for x in (hidden, head_codes, head_scales)))
     steps = 8
     probabilities, entropy = pl.pallas_call(
-        functools.partial(scale_kernel, rows, n_vocab // steps),
+        functools.partial(scale_kernel, rows, n_vocab // steps, n_vocab),
         out_shape=(
             jax.ShapeDtypeStruct((rows, n_vocab * vocab), jnp.bfloat16),
             jax.ShapeDtypeStruct((rows,), jnp.float32),
         ),
-        in_specs=[vmem, vmem],
+        in_specs=[vmem, vmem, vmem],
         out_specs=(hbm, vmem),
         scratch_shapes=[pltpu.VMEM((rows, n_vocab * vocab), jnp.bfloat16), dma((steps,))],
         compiler_params=pltpu.CompilerParams(vmem_limit_bytes=16 << 20),
         name="scale",
-    )(stats, raw)
+    )(entropy, ratio, raw)
     return probabilities, entropy
 
 

time: 105 us -> 103 us (0.981)
  no operation moved by 1% of the time
where the time goes in v3:
time: 103 us
  Pallas kernels  103 us (100%)
    pallas_call x1, Pallas kernels, shards(): pl.pallas_call(functools.partial(head_kernel, rows), out_shape=(jax.Shape...  100 us
    pallas_call x1, Pallas kernels, shards(): pl.pallas_call(functools.partial(scale_kernel, rows, n_vocab // steps, n_...  2.36 us

profile of v3, /device:TPU:1, one launch (start us, length us, event | category | flops | bytes accessed | tf_op | source)
XLA Modules:
  0.0 103.3 jit_solution(2989285132561294818)
XLA Ops:
  0.6 100.3 %head.1 = (bf16[48,32768]{1,0:T(8,128)(2,1)S(1)}, f32[48,128]{1,0:T(8,128)S(1)}, f32[1,128]{1,0:T(1,128)S(1)}) custom-call(bf16[48,7168]{1,0:T(8,128)(2,1)} %hidden.1, bf16[1024,7168]{1,0:T(8,128)(2,1)} %codes.1, f32[8,56]{1,0:T(8,128)} %scales_in.1), custom_call_target="tpu_custom_call" | custom-call | flops 22548578304 | bytes 14680064 | tf_op jit(solution)/shard_map/head/pallas_call | solution.py:289
  100.9 2.4 %scale.1 = (bf16[48,32768]{1,0:T(8,128)(2,1)}, f32[48]{0:T(128)}) custom-call(f32[1,128]{1,0:T(1,128)S(1)} %get-tuple-element.5.entropy_in, f32[48,128]{1,0:T(8,128)S(1)} %get-tuple-element.6.ratio, bf16[48,32768]{1,0:T(8,128)(2,1)S(1)} %get-tuple-element.7.raw), custom_call_target="tpu_custom_call" | custom-call | tf_op jit(solution)/shard_map/scale/pallas_call | solution.py:320

commit v4 on v3

--- a/solution.py
+++ b/solution.py
@@ -100,7 +100,7 @@
                     continue
                 half, chip, quarter = sends[turn]
                 cols = columns(half, quarter)
-                src = hidden.at[:, cols] if chip == (0, 0) else gathered.at[row_block(chip), cols]
+                src = gathered.at[row_block(chip), cols]
                 dst = gathered.at[row_block(add(chip, neg(move))), cols]
                 remote(src, dst, ici_send, ici_recv.at[link * ROUNDS + turn], device(move))
 
@@ -126,6 +126,10 @@
 
     scale_copy = pltpu.make_async_copy(scales_in, scales, scale_sem)
     scale_copy.start()
+    own = (0, 0)
+    own_rows = gathered.at[row_block(own), :]
+    own_copy = pltpu.make_async_copy(hidden, own_rows, copy_sem)
+    own_copy.start()
 
     barrier = pltpu.get_barrier_semaphore()
     neighbours = [device(move) for move, _ in LINKS] + [device((0, 0), 1)]
@@ -133,12 +137,9 @@
         pl.semaphore_signal(barrier, inc=1, device_id=neighbour, device_id_type=MESH)
     pl.semaphore_wait(barrier, len(neighbours))
 
-    own = (0, 0)
+    own_copy.wait()
     send(-1)
-    own_rows = gathered.at[row_block(own), :]
-    remote(hidden, gathered.at[row_block(own, 1), :], sib_send, sib_recv.at[0], device(own, 1))
-    own_copy = pltpu.make_async_copy(hidden, own_rows, copy_sem)
-    own_copy.start()
+    remote(own_rows, gathered.at[row_block(own, 1), :], sib_send, sib_recv.at[0], device(own, 1))
 
     def stage_in(block):
         return pltpu.make_async_copy(
@@ -224,7 +225,6 @@
         if block == 3:
             receive(0)
     receive(1)
-    own_copy.wait()
     compute(STEPS[0], False)
     compute(STEPS[1], False)
     receive(2)

time: 103 us -> 103 us (level)
  no operation moved by 1% of the time
where the time goes in v4:
time: 103 us
  Pallas kernels  102 us (99%)
    pallas_call x1, Pallas kernels, shards(): pl.pallas_call(functools.partial(head_kernel, rows), out_shape=(jax.Shape...  100 us
    pallas_call x1, Pallas kernels, shards(): pl.pallas_call(functools.partial(scale_kernel, rows, n_vocab // steps, n_...  2.36 us

profile of v4, /device:TPU:1, one launch (start us, length us, event | category | flops | bytes accessed | tf_op | source)
XLA Modules:
  0.0 103.0 jit_solution(12714893503107228275)
XLA Ops:
  0.6 100.0 %head.1 = (bf16[48,32768]{1,0:T(8,128)(2,1)S(1)}, f32[48,128]{1,0:T(8,128)S(1)}, f32[1,128]{1,0:T(1,128)S(1)}) custom-call(bf16[48,7168]{1,0:T(8,128)(2,1)} %hidden.1, bf16[1024,7168]{1,0:T(8,128)(2,1)} %codes.1, f32[8,56]{1,0:T(8,128)} %scales_in.1), custom_call_target="tpu_custom_call" | custom-call | flops 22548578304 | bytes 14680064 | tf_op jit(solution)/shard_map/head/pallas_call | solution.py:289
  100.7 2.4 %scale.1 = (bf16[48,32768]{1,0:T(8,128)(2,1)}, f32[48]{0:T(128)}) custom-call(f32[1,128]{1,0:T(1,128)S(1)} %get-tuple-element.5.entropy_in, f32[48,128]{1,0:T(8,128)S(1)} %get-tuple-element.6.ratio, bf16[48,32768]{1,0:T(8,128)(2,1)S(1)} %get-tuple-element.7.raw), custom_call_target="tpu_custom_call" | custom-call | tf_op jit(solution)/shard_map/scale/pallas_call | solution.py:320

commit v5 on v4

--- a/solution.py
+++ b/solution.py
@@ -57,10 +57,11 @@
         for turn, (half, chip, _) in enumerate(sends):
             piece = (half, add(chip, neg(move)))
             here[piece] = max(turn, here.get(piece, 0))
-    return [
+    may = [
         [max(here.get((half, chip), -1), turn - AHEAD if turn > 1 else -1) for turn, (half, chip, _) in enumerate(sends)]
         for _, sends in LINKS
     ]
+    return [[max(turns) for turns in zip(*may)]] * len(LINKS)
 
 
 SEND_TURNS = send_turns()

time: 103 us -> 103 us (level)
  no operation moved by 1% of the time
where the time goes in v5:
time: 103 us
  Pallas kernels  102 us (99%)
    pallas_call x1, Pallas kernels, shards(): pl.pallas_call(functools.partial(head_kernel, rows), out_shape=(jax.Shape...  100 us
    pallas_call x1, Pallas kernels, shards(): pl.pallas_call(functools.partial(scale_kernel, rows, n_vocab // steps, n_...  2.36 us

profile of v5, /device:TPU:1, one launch (start us, length us, event | category | flops | bytes accessed | tf_op | source)
XLA Modules:
  0.0 103.0 jit_solution(7634567682548763612)
XLA Ops:
  0.6 100.0 %head.1 = (bf16[48,32768]{1,0:T(8,128)(2,1)S(1)}, f32[48,128]{1,0:T(8,128)S(1)}, f32[1,128]{1,0:T(1,128)S(1)}) custom-call(bf16[48,7168]{1,0:T(8,128)(2,1)} %hidden.1, bf16[1024,7168]{1,0:T(8,128)(2,1)} %codes.1, f32[8,56]{1,0:T(8,128)} %scales_in.1), custom_call_target="tpu_custom_call" | custom-call | flops 22548578304 | bytes 14680064 | tf_op jit(solution)/shard_map/head/pallas_call | solution.py:290
  100.7 2.4 %scale.1 = (bf16[48,32768]{1,0:T(8,128)(2,1)}, f32[48]{0:T(128)}) custom-call(f32[1,128]{1,0:T(1,128)S(1)} %get-tuple-element.5.entropy_in, f32[48,128]{1,0:T(8,128)S(1)} %get-tuple-element.6.ratio, bf16[48,32768]{1,0:T(8,128)(2,1)S(1)} %get-tuple-element.7.raw), custom_call_target="tpu_custom_call" | custom-call | tf_op jit(solution)/shard_map/scale/pallas_call | solution.py:321

commit v6 on v4

--- a/solution.py
+++ b/solution.py
@@ -63,7 +63,7 @@
     ]
 
 
-SEND_TURNS = send_turns()
+SEND_TURNS = [[max(column) for column in zip(*send_turns(), (-1, -1, 0, 0, 1, 1, 2, 4, 4, 6))]] * len(LINKS)
 
 def head_kernel(
     rows, hidden, codes, scales_in, raw, ratio, entropy,
@@ -234,8 +234,9 @@
     receive(4)
     compute(STEPS[4])
     receive(5)
-    compute(STEPS[5])
+    compute(STEPS[5], False)
     receive(6)
+    deliver_all(STEPS[5])
     receive(7)
     compute(STEPS[6])
     deliver_all([chip for pair in zip(STEPS[1], STEPS[2]) for chip in pair])

time: 103 us -> 103 us (level)
  no operation moved by 1% of the time
where the time goes in v6:
time: 103 us
  Pallas kernels  102 us (99%)
    pallas_call x1, Pallas kernels, shards(): pl.pallas_call(functools.partial(head_kernel, rows), out_shape=(jax.Shape...  100 us
    pallas_call x1, Pallas kernels, shards(): pl.pallas_call(functools.partial(scale_kernel, rows, n_vocab // steps, n_...  2.36 us

profile of v6, /device:TPU:1, one launch (start us, length us, event | category | flops | bytes accessed | tf_op | source)
XLA Modules:
  0.0 103.1 jit_solution(18301240415362969557)
XLA Ops:
  0.6 100.1 %head.1 = (bf16[48,32768]{1,0:T(8,128)(2,1)S(1)}, f32[48,128]{1,0:T(8,128)S(1)}, f32[1,128]{1,0:T(1,128)S(1)}) custom-call(bf16[48,7168]{1,0:T(8,128)(2,1)} %hidden.1, bf16[1024,7168]{1,0:T(8,128)(2,1)} %codes.1, f32[8,56]{1,0:T(8,128)} %scales_in.1), custom_call_target="tpu_custom_call" | custom-call | flops 22548578304 | bytes 14680064 | tf_op jit(solution)/shard_map/head/pallas_call | solution.py:290
  100.7 2.4 %scale.1 = (bf16[48,32768]{1,0:T(8,128)(2,1)}, f32[48]{0:T(128)}) custom-call(f32[1,128]{1,0:T(1,128)S(1)} %get-tuple-element.5.entropy_in, f32[48,128]{1,0:T(8,128)S(1)} %get-tuple-element.6.ratio, bf16[48,32768]{1,0:T(8,128)(2,1)S(1)} %get-tuple-element.7.raw), custom_call_target="tpu_custom_call" | custom-call | tf_op jit(solution)/shard_map/scale/pallas_call | solution.py:321
